TPU v7x, 128 devices: a whole 4x4x4 slice. The times are simulated.
128 devices in a mesh: grp: 8 (over x, y_lo), loss: 16 (over z, y_hi, core).
Axes of the slice: x: 4, y: 4 (y_hi: 2, y_lo: 2; y = y_hi * 2 + y_lo), z: 4, core: 2. Of those that a mesh axis runs over, the one named last changes fastest.
Arguments:
- image_embeds: bfloat16 [65536, 1152], P(('grp', 'loss')), parts along dimension 0, may hold values from -0.8 to 0.8
- text_embeds: bfloat16 [65536, 1152], P(('grp', 'loss')), parts along dimension 0, may hold values from -0.8 to 0.8
- log_scale: float32 [8], P('grp'), parts along dimension 0, may hold values from 2 to 2.5
- bias: float32 [8], P('grp'), parts along dimension 0, may hold values from -3 to -1
Outputs:
- loss_rows: float32 [65536], P(('grp', 'loss')), parts along dimension 0
- grad_image: bfloat16 [65536, 1152], P(('grp', 'loss')), parts along dimension 0
- grad_text: bfloat16 [65536, 1152], P(('grp', 'loss')), parts along dimension 0
There are 8 independent parts, one for each index of `grp`. A program takes and returns all parts, laid end to end along the dimension named above; each array names one. Nothing has to cross between parts.
All inputs are finite; a program needn't handle non-finite values.
Results may differ from a plain program's by a relative error of at most 0.0034.
Values may be sent and summed in bfloat16 or wider, within the bound.
No kernel may reach another device: no remote copies, remote signals or barrier semaphores. Data moves between devices by JAX's collectives and lax.ppermute only.
A program may use at most 192 MiB of HBM per device.

v0:
```python
import jax
import jax.numpy as jnp
from jax import lax
from jax.sharding import PartitionSpec as P


def normalize(raw):
    wide = raw.astype(jnp.float32)
    recip = lax.rsqrt(jnp.sum(wide * wide, axis=1, keepdims=True) + 1e-06)
    return (wide * recip, recip)


def tangent(grad_unit, unit, recip):
    along = jnp.sum(unit * grad_unit, axis=1, keepdims=True)
    return ((grad_unit - unit * along) * recip).astype(jnp.bfloat16)


def per_device(image_embeds, text_embeds, log_scale, bias):
    rows = image_embeds.shape[0]
    group = lax.axis_size("loss")
    total = rows * group
    scale = jnp.exp(log_scale[0])
    offset = bias[0]
    img_unit, img_recip = normalize(image_embeds)
    txt_unit, txt_recip = normalize(text_embeds)
    img_half = img_unit.astype(jnp.bfloat16)
    txt_half = txt_unit.astype(jnp.bfloat16)
    position = lax.axis_index("loss")
    own_rows = position * rows + jnp.arange(rows, dtype=jnp.int32)
    piece = lax.all_gather(txt_half, "loss", axis=0, tiled=True)
    count = piece.shape[0]
    logits = (
        scale
        * lax.dot_general(
            img_half, piece, (((1,), (1,)), ((), ())), preferred_element_type=jnp.float32
        )
        + offset
    )
    columns = jnp.arange(count, dtype=jnp.int32)
    diagonal = own_rows[:, None] == columns[None, :]
    signs = jnp.where(diagonal, 1.0, -1.0).astype(jnp.float32)
    loss_part = jnp.sum(jax.nn.softplus(-signs * logits), axis=1)
    weights = (jax.nn.sigmoid(logits) - diagonal.astype(jnp.float32)).astype(jnp.bfloat16)
    weights, loss_part = (weights, loss_part)
    grad_sum = jnp.dot(weights, piece, preferred_element_type=jnp.float32)
    loss_sum = loss_part
    grad_sum, loss_sum, all_weights = (grad_sum, loss_sum, weights)
    grad_txt_unit = lax.psum_scatter(
        scale
        * lax.dot_general(
            all_weights, img_half, (((0,), (0,)), ((), ())), preferred_element_type=jnp.float32
        ),
        "loss",
        scatter_dimension=0,
        tiled=True,
    )
    loss_rows = loss_sum / total
    grad_image = tangent(scale * grad_sum, img_unit, img_recip)
    grad_text = tangent(grad_txt_unit, txt_unit, txt_recip)
    return (loss_rows, grad_image, grad_text)


def solution(mesh):
    placed = (P(("grp", "loss"), None), P(("grp", "loss"), None), P("grp"), P("grp"))
    return jax.shard_map(
        per_device,
        mesh=mesh,
        in_specs=placed,
        out_specs=(P(("grp", "loss")), P(("grp", "loss"), None), P(("grp", "loss"), None)),
        check_vma=False,
    )
```

profile of v0, /device:TPU:0, one launch (start us, length us, event | category | flops | bytes accessed | tf_op | source)
XLA Modules:
  0.0 459.8 jit_solution(14761250485500711176)
XLA Ops:
  7.2 0.0 copy-start.2
  7.2 0.0 all-gather.2.cloned.1.call-start
  7.2 1.7 fusion.16
  8.9 2.6 fusion.3
  11.4 0.0 all-gather.2.cloned.1.call-update
  11.5 0.0 reduce-scatter.2.cloned.1.call-start
  12.9 0.0 copy-done.2
  12.9 0.3 fusion.11
  13.2 119.9 %all-gather.2.cloned.1.call-done = bf16[8192,1152]{1,0:T(8,128)(2,1)} async-done(((bf16[512,1152]{1,0:T(8,128)(2,1)}), bf16[8192,1152]{1,0:T(8,128)(2,1)}) %all-gather.2.cloned.1.call-update) | async-done | bytes 18874384 | tf_op jit(solution)/shard_map/all_gather | solution.py:30
  133.1 27.0 %fusion = (f32[512]{0:T(512)S(1)}, f32[512,8192]{1,0:T(8,128)}) fusion(f32[]{:T(128)} %bitcast.4, f32[]{:T(128)} %bitcast, s32[512]{0:T(512)S(1)} %iota_add_fusion, bf16[8192,1152]{1,0:T(8,128)(2,1)} %all-gather.2.cloned.1.call-done, bf16[512,1152]{1,0:T(8,128)(2,1)S(1)} %copy-done.2, f32[512]{0:T(512)S(1)} %add_rsqrt_fusion.1), kind=kOutput, calls=%fused_computation.2 | convolution fusion | flops 9719971840 | bytes 36837384 | tf_op jit(solution)/shard_map/dot_general | solution.py:34
  160.1 24.4 %convolution_multiply_fusion = f32[8192,1152]{1,0:T(8,128)} fusion(f32[]{:T(128)} %bitcast, bf16[512,1152]{1,0:T(8,128)(2,1)S(1)} %copy-done.2, f32[512]{0:T(512)S(1)} %add_rsqrt_fusion.1, f32[512,8192]{1,0:T(8,128)} %get-tuple-element.4, f32[]{:T(128)} %bitcast.6, s32[512]{0:T(512)S(1)} %iota_add_fusion), kind=kOutput, calls=%fused_computation.1 | convolution fusion | flops 9712631808 | bytes 55709704 | tf_op jit(solution)/shard_map/dot_general | solution.py:50
  184.5 0.0 reduce-scatter.2.cloned.1.call-update
  184.5 0.6 broadcast_multiply_fusion
  185.1 24.2 %fusion.7 = (f32[512]{0:T(512)S(1)}, f32[512,1152]{1,0:T(8,128)S(1)}) fusion(bf16[512,1152]{1,0:T(8,128)(2,1)S(1)} %copy-done.2, f32[512]{0:T(512)S(1)} %add_rsqrt_fusion.1, bf16[8192,1152]{1,0:T(8,128)(2,1)} %all-gather.2.cloned.1.call-done, f32[512,8192]{1,0:T(8,128)} %get-tuple-element.4, f32[]{:T(128)} %bitcast.5, f32[]{:T(128)} %bitcast, ...), kind=kOutput, calls=%fused_computation.17 | convolution fusion | flops 9704374272 | bytes 39196680 | tf_op jit(solution)/shard_map/dot_general | solution.py:45
  209.3 0.0 copy-start
  209.3 1.5 fusion.10
  210.8 238.3 %reduce-scatter.2.cloned.1.call-done = f32[512,1152]{1,0:T(8,128)} async-done(((f32[8192,1152]{1,0:T(8,128)}), f32[512,1152]{1,0:T(8,128)}) %reduce-scatter.2.cloned.1.call-update) | async-done | bytes 2359312 | tf_op jit(solution)/shard_map/reduce_scatter | solution.py:48
  449.1 0.0 copy-done
  449.1 0.0 copy-start.1
  449.1 2.3 fusion.12
  451.4 0.1 copy-done.1
  451.5 1.5 fusion.15
  (3 shorter events, 0.0 us)
Async XLA Ops:
  7.2 5.7 %copy-start.2 = (bf16[512,1152]{1,0:T(8,128)(2,1)S(1)}, bf16[512,1152]{1,0:T(8,128)(2,1)}, u32[]{:S(2)}) copy-start(bf16[512,1152]{1,0:T(8,128)(2,1)} %param.4) | copy-start | bytes 3538948
  7.2 125.9 %all-gather.2.cloned.1.call-start = ((), (), s32[]{:S(2)}) async-start(), calls=%async_computation.1 | async-start | bytes 20054016 | tf_op jit(solution)/shard_map/all_gather | solution.py:30
  11.5 437.6 %reduce-scatter.2.cloned.1.call-start = ((), (), s32[]{:S(2)}) async-start(), calls=%async_computation.2 | async-start | bytes 40108032 | tf_op jit(solution)/shard_map/reduce_scatter | solution.py:48
  209.3 239.8 %copy-start = (bf16[512,1152]{1,0:T(8,128)(2,1)S(1)}, bf16[512,1152]{1,0:T(8,128)(2,1)}, u32[]{:S(2)}) copy-start(bf16[512,1152]{1,0:T(8,128)(2,1)} %param.5) | copy-start | bytes 3538948
  449.1 2.4 copy-start.1
Sparse Core Ops, SparseCore 0:
  11.6 121.4 all-gather.1
  184.7 264.4 reduce-scatter.1
where the time goes:
time: 460 us
  waiting for transfers between devices  358 us (78%)
  matrix products  75.6 us (16%)
  between operations  15.4 us (3%)
  other arithmetic  10.4 us (2%)
    reduce_scatter x1, waiting for transfers between devices, per_device(): lax.psum_scatter(scale * lax.dot_general(all_weights, img_half, (((0,), (...  238 us
    all_gather x1, waiting for transfers between devices, per_device(): piece = lax.all_gather(txt_half, 'loss', axis=0, tiled=True)  120 us
    dot_general x1, matrix products, per_device(): lax.dot_general(img_half, piece, (((1,), (1,)), ((), ())), preferred_elem...  27 us
    dot_general x1, matrix products, per_device(): lax.dot_general(all_weights, img_half, (((0,), (0,)), ((), ())), preferre...  24.4 us
    dot_general x1, matrix products, per_device(): grad_sum = jnp.dot(weights, piece, preferred_element_type=jnp.float32)  24.2 us
  transfers between devices with their start and end apart: 2, of which 2 were waited for; matrix products, arithmetic and copies ran while one was open for 6% of the time, Pallas kernels for 0%

commit v1 on v0

v1 whole, which is shorter than its diff:
```python
import functools
import math

import jax
import jax.numpy as jnp
from jax import lax
from jax.experimental import pallas as pl
from jax.experimental.pallas import tpu as pltpu
from jax.sharding import PartitionSpec as P

BF, F32 = jnp.bfloat16, jnp.float32
ANY = pl.BlockSpec(memory_space=pl.ANY)
SMEM = pl.BlockSpec(memory_space=pltpu.SMEM)
VMEM = pl.BlockSpec(memory_space=pltpu.VMEM)
PAD = 16
PARAMS = pltpu.CompilerParams(vmem_limit_bytes=56 * 2**20)
NT = (((1,), (1,)), ((), ()))
TN = (((0,), (0,)), ((), ()))


def recip_of(wide):
    return lax.rsqrt(jnp.sum(wide * wide, axis=1, keepdims=True) + 1e-06)


def normalize_kernel(a_ref, b_ref, oa_ref, ob_ref):
    for ref, out in ((a_ref, oa_ref), (b_ref, ob_ref)):
        wide = ref[...].astype(F32)
        out[...] = (wide * recip_of(wide)).astype(BF)


def normalize(a, b):
    rows, width = a.shape
    spec = pl.BlockSpec((rows // 2, width), lambda i: (i, 0))
    return pl.pallas_call(
        normalize_kernel,
        grid=(2,),
        in_specs=[spec, spec],
        out_specs=[spec, spec],
        out_shape=[jax.ShapeDtypeStruct(a.shape, BF)] * 2,
        compiler_params=PARAMS,
    )(a, b)


def pair_terms(logits, scale, bias, flip):
    z = logits * scale + bias
    if flip is not None:
        z = z * flip
    e = jnp.exp2(z)
    u = 1.0 + e
    w = e * pl.reciprocal(u, approx=True)
    if flip is not None:
        w = w * flip
    q = logits.shape[1] // 4
    e0, e1, e2, e3 = (e[:, k * q : (k + 1) * q] for k in range(4))
    u0, u1, u2 = (u[:, k * q : (k + 1) * q] for k in range(3))
    s = (e0 + e1 * u0) + (e2 + e3 * u2) * (u0 * u1)
    terms = jnp.log1p(s)
    total = terms[:, :128]
    for k in range(1, q // 128):
        total = total + terms[:, k * 128 : (k + 1) * 128]
    return w.astype(BF), total


def rows_kernel(n_i, n_t, own, far, scal, *refs):
    i_in, t_in = refs[:n_i], refs[n_i : n_i + n_t]
    outs = refs[n_i + n_t : n_i + n_t + 3]
    i_buf, t_buf, w_buf, ga_buf, gb_buf, in_sem, out_sem = refs[n_i + n_t + 3 :]
    rows, width = i_buf.shape
    block = t_buf.shape[0] // n_t
    part = rows // n_i
    w_out = outs[0]
    i_copies = [
        pltpu.make_async_copy(i_in[k], i_buf.at[pl.ds(k * part, part), :], in_sem.at[k]) for k in range(n_i)
    ]
    t_copies = [
        pltpu.make_async_copy(t_in[k], t_buf.at[pl.ds(k * block, block), :], in_sem.at[n_i + k])
        for k in range(n_t)
    ]
    for c in i_copies + t_copies:
        c.start()
    for c in i_copies:
        c.wait()
    a = i_buf[...]
    scale, bias = scal[0], scal[1]
    acc = loss = None
    w_copies = []
    for k in range(n_t):
        t_copies[k].wait()
        t = t_buf[k * block : (k + 1) * block, :]
        logits = lax.dot_general(a, t, NT, preferred_element_type=F32)
        flip = None
        if own and k == 0:
            r = lax.broadcasted_iota(jnp.int32, logits.shape, 0)
            c = lax.broadcasted_iota(jnp.int32, logits.shape, 1)
            flip = jnp.where(r == c, -1.0, 1.0).astype(F32)
        w, lane = pair_terms(logits, scale, bias, flip)
        w_buf[:, k * block : (k + 1) * block] = w
        cols = pl.ds(k * block, block)
        w_copies.append(pltpu.make_async_copy(w_buf.at[:, cols], w_out.at[:, cols], out_sem.at[k]))
        w_copies[-1].start()
        prod = jnp.dot(w, t, preferred_element_type=F32)
        acc = prod if acc is None else acc + prod
        loss = lane if loss is None else loss + lane
    line = jnp.sum(jnp.transpose(loss), axis=0, keepdims=True)
    if own:
        ga_buf[...] = acc
        gb_buf[...] = jnp.broadcast_to(line, gb_buf.shape)
    else:
        half = rows // 2
        r = lax.broadcasted_iota(jnp.int32, (PAD, width), 0)
        first = 2 if far else 0
        for k, buf in enumerate((ga_buf, gb_buf)):
            buf[:half, :] = acc[k * half : (k + 1) * half].astype(BF)
            piece = line[:, k * half : (k + 1) * half]
            hi = piece.astype(BF).astype(F32)
            blank = jnp.zeros((1, width - half), F32)
            hi_row = jnp.concatenate([hi, blank], axis=1)
            lo_row = jnp.concatenate([piece - hi, blank], axis=1)
            pad = jnp.where(r == first, hi_row, jnp.where(r == first + 1, lo_row, 0.0))
            buf[half:, :] = pad.astype(BF)
    g_copies = [
        pltpu.make_async_copy(ga_buf, outs[1], out_sem.at[n_t]),
        pltpu.make_async_copy(gb_buf, outs[2], out_sem.at[n_t + 1]),
    ]
    for c in g_copies:
        c.start()
    for c in w_copies + g_copies:
        c.wait()


def rows_step(scal, pieces, texts, own=False, far=False):
    width = pieces[0].shape[1]
    rows = sum(p.shape[0] for p in pieces)
    cols = sum(t.shape[0] for t in texts)
    n_i, n_t = len(pieces), len(texts)
    if own:
        grads = [jax.ShapeDtypeStruct((rows, width), F32), jax.ShapeDtypeStruct((8, rows), F32)]
    else:
        grads = [jax.ShapeDtypeStruct((rows // 2 + PAD, width), BF)] * 2
    return pl.pallas_call(
        functools.partial(rows_kernel, n_i, n_t, own, far),
        in_specs=[SMEM] + [ANY] * (n_i + n_t),
        out_specs=[ANY] * 3,
        out_shape=[jax.ShapeDtypeStruct((rows, cols), BF)] + grads,
        scratch_shapes=[
            pltpu.VMEM((rows, width), BF),
            pltpu.VMEM((cols, width), BF),
            pltpu.VMEM((rows, cols), BF),
            pltpu.VMEM(grads[0].shape, grads[0].dtype),
            pltpu.VMEM(grads[1].shape, grads[1].dtype),
            pltpu.SemaphoreType.DMA((n_i + n_t,)),
            pltpu.SemaphoreType.DMA((n_t + 2,)),
        ],
        compiler_params=PARAMS,
    )(scal, *pieces, *texts)


def cols_kernel(n_w, n_i, first, wide, *refs):
    w_in, i_in = refs[:n_w], refs[n_w : n_w + n_i]
    outs = refs[n_w + n_i : n_w + n_i + 2]
    w_buf, i_buf, oa_buf, ob_buf, in_sem, out_sem = refs[n_w + n_i + 2 :]
    rows = w_buf.shape[1]
    block = w_buf.shape[2] // 2
    w_copies = [
        pltpu.make_async_copy(w_in[k].at[:, pl.ds(first, 2 * block)], w_buf.at[k], in_sem.at[k])
        for k in range(n_w)
    ]
    i_copies, at = [], 0
    for k in range(n_i):
        size = i_in[k].shape[0]
        i_copies.append(
            pltpu.make_async_copy(i_in[k], i_buf.at[pl.ds(at, size), :], in_sem.at[n_w + k])
        )
        at += size
    for c in w_copies + i_copies:
        c.start()
    for c in w_copies + i_copies:
        c.wait()
    out_copies = []
    for h, buf in enumerate((oa_buf, ob_buf)):
        acc = None
        for k in range(n_w):
            prod = lax.dot_general(
                w_buf[k, :, h * block : (h + 1) * block],
                i_buf[k * rows : (k + 1) * rows, :],
                TN,
                preferred_element_type=F32,
            )
            acc = prod if acc is None else acc + prod
        buf[...] = acc.astype(buf.dtype)
        out_copies.append(pltpu.make_async_copy(buf, outs[h], out_sem.at[h]))
        out_copies[-1].start()
    for c in out_copies:
        c.wait()


def cols_step(weights, images, first, dtypes):
    width = images[0].shape[1]
    rows = weights[0].shape[0]
    total = sum(i.shape[0] for i in images)
    block = weights[0].shape[1] // 4
    n_w, n_i = len(weights), len(images)
    shapes = [jax.ShapeDtypeStruct((block, width), d) for d in dtypes]
    return pl.pallas_call(
        functools.partial(cols_kernel, n_w, n_i, first * block, None),
        in_specs=[ANY] * (n_w + n_i),
        out_specs=[ANY] * 2,
        out_shape=shapes,
        scratch_shapes=[
            pltpu.VMEM((n_w, rows, 2 * block), BF),
            pltpu.VMEM((total, width), BF),
            pltpu.VMEM(shapes[0].shape, shapes[0].dtype),
            pltpu.VMEM(shapes[1].shape, shapes[1].dtype),
            pltpu.SemaphoreType.DMA((n_w + n_i,)),
            pltpu.SemaphoreType.DMA((2,)),
        ],
        compiler_params=PARAMS,
    )(*weights, *images)


def tangent(total, raw):
    wide = raw.astype(F32)
    recip = recip_of(wide)
    unit = wide * recip
    along = jnp.sum(unit * total, axis=1, keepdims=True)
    return ((total - unit * along) * recip).astype(BF)


def image_kernel(count, scal, raw, own, loss, s_ref, r_ref, grad_ref, loss_ref):
    rows = raw.shape[0]
    total = own[...] + s_ref[:rows, :].astype(F32) + r_ref[:rows, :].astype(F32)
    grad_ref[...] = tangent(total * scal[2], raw[...])
    tail = s_ref[rows:, :rows].astype(F32) + r_ref[rows:, :rows].astype(F32)
    loss_ref[...] = (loss[...] + jnp.sum(tail, axis=0, keepdims=True)) * (1.0 / count)


def image_step(scal, raw, own, loss, summed, near, half, count):
    rows, width = raw.shape
    part = rows // 2
    mine = pl.BlockSpec((part, width), lambda i: (half, 0))
    whole = pl.BlockSpec((part + PAD, width), lambda i: (0, 0))
    line = pl.BlockSpec((8, part), lambda i: (0, half))
    return pl.pallas_call(
        functools.partial(image_kernel, count),
        grid=(1,),
        in_specs=[SMEM, mine, mine, line, whole, whole],
        out_specs=[pl.BlockSpec((part, width), lambda i: (0, 0)), pl.BlockSpec((8, part), lambda i: (0, 0))],
        out_shape=[jax.ShapeDtypeStruct((part, width), BF), jax.ShapeDtypeStruct((8, part), F32)],
        compiler_params=PARAMS,
    )(scal, raw, own, loss, summed, near)


def text_kernel(scal, raw, own, a_ref, b_ref, grad_ref):
    total = own[...] + a_ref[...].astype(F32) + b_ref[...].astype(F32)
    grad_ref[...] = tangent(total * scal[2], raw[...])


def text_step(scal, raw, own, a, b):
    rows, width = raw.shape
    spec = pl.BlockSpec((rows // 2, width), lambda i: (i, 0))
    return pl.pallas_call(
        text_kernel,
        grid=(2,),
        in_specs=[SMEM] + [spec] * 4,
        out_specs=spec,
        out_shape=jax.ShapeDtypeStruct((rows, width), BF),
        compiler_params=PARAMS,
    )(scal, raw, own, a, b)


def per_device(total, image_embeds, text_embeds, log_scale, bias):
    def move(value, dz=0, dy=0, dc=0):
        pairs = [
            (z * 4 + y * 2 + c, (z + dz) % 4 * 4 + (y + dy) % 2 * 2 + (c + dc) % 2)
            for z in range(4)
            for y in range(2)
            for c in range(2)
        ]
        return lax.ppermute(value, "loss", pairs)

    scale = jnp.exp(log_scale[0])
    scal = jnp.stack([scale * (1.0 / math.log(2.0)), bias[0] * (1.0 / math.log(2.0)), scale])
    img, txt = normalize(image_embeds, text_embeds)
    half = img.shape[0] // 2
    a, b = img[:half], img[half:]
    prev_a, next_b = move(a, dz=1), move(b, dz=-1)
    txt_y = move(txt, dy=1)
    txt_c = move(txt, dc=1)
    far_a, far_b = move(prev_a, dz=1), move(next_b, dz=-1)
    txt_yc = move(txt_y, dc=1)
    prev_b, next_a = move(b, dz=1), move(a, dz=-1)
    texts = [txt, txt_c, txt_y, txt_yc]

    w_own, g_own, l_own = rows_step(scal, [img], texts, own=True)
    w_first, g_prev_a, g_next_b = rows_step(scal, [prev_a, next_b], texts)
    w_far, g_far_a, g_far_b = rows_step(scal, [far_a, far_b], texts, far=True)
    w_last, g_prev_b, g_next_a = rows_step(scal, [prev_b, next_a], texts)

    through_a, through_b = move(g_far_a, dz=-1), move(g_far_b, dz=1)
    near_b, near_a = move(g_prev_b, dz=-1), move(g_next_a, dz=1)
    sum_a = move(g_prev_a + through_a, dz=-1)
    sum_b = move(g_next_b + through_b, dz=1)

    weights = [w_own, w_first, w_far, w_last]
    images = [img, prev_a, next_b, far_a, far_b, prev_b, next_a]
    gt_y, gt_yc = cols_step(weights, images, 2, (BF, BF))
    text_y = move(gt_y + move(gt_yc, dc=1), dy=1)
    gt_own, gt_c = cols_step(weights, images, 0, (F32, BF))
    text_c = move(gt_c, dc=1)

    grad_a, loss_a = image_step(scal, image_embeds, g_own, l_own, sum_a, near_a, 0, total)
    grad_b, loss_b = image_step(scal, image_embeds, g_own, l_own, sum_b, near_b, 1, total)
    grad_text = text_step(scal, text_embeds, gt_own, text_c, text_y)
    loss_rows = jnp.concatenate([loss_a[0], loss_b[0]])
    return loss_rows, jnp.concatenate([grad_a, grad_b]), grad_text


def solution(mesh):
    placed = (P(("grp", "loss"), None), P(("grp", "loss"), None), P("grp"), P("grp"))

    def whole(image_embeds, text_embeds, log_scale, bias):
        total = image_embeds.shape[0] // mesh.shape["grp"]
        return jax.shard_map(
            functools.partial(per_device, total),
            mesh=mesh,
            in_specs=placed,
            out_specs=(P(("grp", "loss")), P(("grp", "loss"), None), P(("grp", "loss"), None)),
            check_vma=False,
        )(image_embeds, text_embeds, log_scale, bias)

    return whole
```

time: 460 us -> 187 us (0.41)
  waiting for transfers between devices: 358 us -> 59.6 us
  Pallas kernels: 0 us -> 80.7 us
  matrix products: 75.6 us -> 0 us
  starting transfers between devices: 0.08 us -> 26 us
  between operations: 15.4 us -> 2.43 us
  local copies, waits for them, and re-layouts: 0.1 us -> 10.9 us
  other arithmetic: 10.4 us -> 3.94 us
    reduce_scatter x1 -> x0, waiting for transfers between devices: 238 us -> none  [per_device(): lax.psum_scatter(scale * lax.dot_general(all_weights, img_half, (((0,), (...]
    all_gather x1 -> x0, waiting for transfers between devices: 120 us -> none  [per_device(): piece = lax.all_gather(txt_half, 'loss', axis=0, tiled=True)]
    pallas_call x0 -> x10, Pallas kernels: none -> 80.7 us  [the longest x4 46.2 us: rows_step(): pl.pallas_call(functools.partial(rows_kernel, n_i, n_t, own, far), in_spe...]
    dot_general x3 -> x0, matrix products: 75.6 us -> none  [the longest x1 27 us: per_device(): lax.dot_general(img_half, piece, (((1,), (1,)), ((), ())), preferred_elem...]
    ppermute x0 -> x18, waiting for transfers between devices: none -> 59.6 us  [move(): return lax.ppermute(value, 'loss', pairs)]
    ppermute x0 -> x18, starting transfers between devices: none -> 26 us  [move(): return lax.ppermute(value, 'loss', pairs)]
    unnamed x6 -> x42, local copies, waits for them, and re-layouts: 0.1 us -> 8.22 us
    convert_element_type x3 -> x0, other arithmetic: 5.59 us -> none  [the longest x2 3.04 us: tangent(): return ((grad_unit - unit * along) * recip).astype(jnp.bfloat16)]
  transfers between devices with their start and end apart: 2 -> 18, of which waited for: 2 -> 6; matrix products, arithmetic and copies ran while one was open for 6% -> 4% of each run, Pallas kernels for 0% -> 28%
where the time goes in v1:
time: 187 us; the launch traced here: 184 us
  Pallas kernels  80.7 us (43%)
  waiting for transfers between devices  59.6 us (32%)
  starting transfers between devices  26 us (14%)
  local copies, waits for them, and re-layouts  10.9 us (6%)
  other arithmetic  3.94 us (2%)
  between operations  2.43 us (1%)
    ppermute x18, waiting for transfers between devices, move(): return lax.ppermute(value, 'loss', pairs)  59.6 us
    pallas_call x4, Pallas kernels, rows_step(): pl.pallas_call(functools.partial(rows_kernel, n_i, n_t, own, far), in_spe...  46.2 us
    ppermute x18, starting transfers between devices, move(): return lax.ppermute(value, 'loss', pairs)  26 us
    pallas_call x2, Pallas kernels, cols_step(): pl.pallas_call(functools.partial(cols_kernel, n_w, n_i, first * block, No...  21 us
    unnamed x42, local copies, waits for them, and re-layouts  8.22 us
    pallas_call x2, Pallas kernels, image_step(): pl.pallas_call(functools.partial(image_kernel, count), grid=(1,), in_spec...  6.49 us
    pallas_call x1, Pallas kernels, text_step(): pl.pallas_call(text_kernel, grid=(2,), in_specs=[SMEM] + [spec] * 4, out_...  4.06 us
  transfers between devices with their start and end apart: 18, of which 6 were waited for; matrix products, arithmetic and copies ran while one was open for 4% of the time, Pallas kernels for 28%

profile of v1, /device:TPU:0, one launch (start us, length us, event | category | flops | bytes accessed | tf_op | source)
XLA Modules:
  0.0 183.7 jit_solution(17663969889459186738)
XLA Ops:
  0.6 2.9 %shard_map.67 = (bf16[512,1152]{1,0:T(8,128)(2,1)}, bf16[512,1152]{1,0:T(8,128)(2,1)}) custom-call(bf16[512,1152]{1,0:T(8,128)(2,1)} %raw.4, bf16[512,1152]{1,0:T(8,128)(2,1)} %raw.5), custom_call_target="tpu_custom_call" | custom-call | tf_op jit(solution)/shard_map/pallas_call | solution.py:34
  3.6 3.3 %collective-permute-start.1 = (bf16[512,1152]{1,0:T(8,128)(2,1)}, bf16[512,1152]{1,0:T(8,128)(2,1)S(1)}, u32[]{:S(2)}, u32[]{:S(2)}) collective-permute-start(bf16[512,1152]{1,0:T(8,128)(2,1)} %get-tuple-element.26.refs_1_.refs_2_), channel_id=1, source_target_pairs={{0,2},{1,3},{2,0},{3,1},{4,6},{5,7},{6,4},{7,5},{8,10},{9,11},{10,... | collective-permute-start | bytes 3538952 | tf_op jit(solution)/shard_map/ppermute | solution.py:279
  6.9 1.3 fusion
  8.2 24.8 %collective-permute-done.1.refs_3_.refs_4_ = bf16[512,1152]{1,0:T(8,128)(2,1)S(1)} collective-permute-done((bf16[512,1152]{1,0:T(8,128)(2,1)}, bf16[512,1152]{1,0:T(8,128)(2,1)S(1)}, u32[]{:S(2)}, u32[]{:S(2)}) %collective-permute-start.1) | collective-permute-done | bytes 1179680 | tf_op jit(solution)/shard_map/ppermute | solution.py:279
  33.0 2.0 %collective-permute-start.3 = (bf16[256,1152]{1,0:T(8,128)(2,1)S(1)}, bf16[256,1152]{1,0:T(8,128)(2,1)S(1)}, u32[]{:S(2)}, u32[]{:S(2)}) collective-permute-start(bf16[256,1152]{1,0:T(8,128)(2,1)S(1)} %get-tuple-element.48), channel_id=1, source_target_pairs={{0,4},{1,5},{2,6},{3,7},{4,8},{5,9},{6,10},{7,11},{8,12},{9,13},{1... | collective-permute-start | bytes 1769480 | tf_op jit(solution)/shard_map/ppermute | solution.py:279
  35.0 2.2 %collective-permute-start.4 = (bf16[256,1152]{1,0:T(8,128)(2,1)S(1)}, bf16[256,1152]{1,0:T(8,128)(2,1)S(1)}, u32[]{:S(2)}, u32[]{:S(2)}) collective-permute-start(bf16[256,1152]{1,0:T(8,128)(2,1)S(1)} %get-tuple-element.47), channel_id=1, source_target_pairs={{0,12},{1,13},{2,14},{3,15},{4,0},{5,1},{6,2},{7,3},{8,4},{9,5},{1... | collective-permute-start | bytes 1769480 | tf_op jit(solution)/shard_map/ppermute | solution.py:279
  37.2 13.9 %collective-permute-done.3.refs_0_.refs_5_ = bf16[256,1152]{1,0:T(8,128)(2,1)S(1)} collective-permute-done((bf16[256,1152]{1,0:T(8,128)(2,1)S(1)}, bf16[256,1152]{1,0:T(8,128)(2,1)S(1)}, u32[]{:S(2)}, u32[]{:S(2)}) %collective-permute-start.3) | collective-permute-done | bytes 589856 | tf_op jit(solution)/shard_map/ppermute | solution.py:279
  51.1 3.2 %collective-permute-start.6 = (bf16[256,1152]{1,0:T(8,128)(2,1)S(1)}, bf16[256,1152]{1,0:T(8,128)(2,1)S(1)}, u32[]{:S(2)}, u32[]{:S(2)}) collective-permute-start(bf16[256,1152]{1,0:T(8,128)(2,1)S(1)} %collective-permute-done.4.refs_1_.refs_6_), channel_id=1, source_target_pairs={{0,12},{1,13},{2,14},{3,15},{4,0},{5,1},{6,2},{7,3},{8,4},{9,5},{1... | collective-permute-start | bytes 1769480 | tf_op jit(solution)/shard_map/ppermute | solution.py:279
  54.4 3.4 %collective-permute-start.10 = (bf16[256,1152]{1,0:T(8,128)(2,1)S(1)}, bf16[256,1152]{1,0:T(8,128)(2,1)S(1)}, u32[]{:S(2)}, u32[]{:S(2)}) collective-permute-start(bf16[256,1152]{1,0:T(8,128)(2,1)S(1)} %get-tuple-element.48), channel_id=1, source_target_pairs={{0,12},{1,13},{2,14},{3,15},{4,0},{5,1},{6,2},{7,3},{8,4},{9,5},{1... | collective-permute-start | bytes 1769480 | tf_op jit(solution)/shard_map/ppermute | solution.py:279
  59.1 0.6 pad_maximum_fusion.2.scal
  59.7 1.0 copy-done.2
  60.7 11.8 %shard_map.68 = (bf16[512,2048]{1,0:T(8,128)(2,1)}, f32[512,1152]{1,0:T(8,128)}, f32[8,512]{1,0:T(8,128)}) custom-call(f32[3]{0:T(128)} %pad_maximum_fusion.2.scal, bf16[512,1152]{1,0:T(8,128)(2,1)} %get-tuple-element.25.refs_0_.refs_4_, bf16[512,1152]{1,0:T(8,128)(2,1)} %get-tuple-element.26.refs_1_.refs_2_, bf16[512,1152]{1,0:T(8,128)(2,1)} %copy-done.1, ...), custom_call_target="tpu_custom_call" | custom-call | tf_op jit(solution)/shard_map/pallas_call | solution.py:140
  72.6 11.3 %shard_map.69 = (bf16[512,2048]{1,0:T(8,128)(2,1)}, bf16[272,1152]{1,0:T(8,128)(2,1)}, bf16[272,1152]{1,0:T(8,128)(2,1)}) custom-call(f32[3]{0:T(128)} %pad_maximum_fusion.2.scal, bf16[256,1152]{1,0:T(8,128)(2,1)} %copy-done.3, bf16[256,1152]{1,0:T(8,128)(2,1)} %copy-done.4, bf16[512,1152]{1,0:T(8,128)(2,1)} %get-tuple-element.26.refs_1_.refs_2_, ...), custom_call_target="tpu_custom_call" | custom-call | tf_op jit(solution)/shard_map/pallas_call | solution.py:140
  83.9 0.8 copy-done.5
  84.7 0.8 copy-done.6
  85.6 11.7 %shard_map.70 = (bf16[512,2048]{1,0:T(8,128)(2,1)}, bf16[272,1152]{1,0:T(8,128)(2,1)}, bf16[272,1152]{1,0:T(8,128)(2,1)}) custom-call(f32[3]{0:T(128)} %pad_maximum_fusion.2.scal, bf16[256,1152]{1,0:T(8,128)(2,1)} %copy-done.5, bf16[256,1152]{1,0:T(8,128)(2,1)} %copy-done.6, bf16[512,1152]{1,0:T(8,128)(2,1)} %get-tuple-element.26.refs_1_.refs_2_, ...), custom_call_target="tpu_custom_call" | custom-call | tf_op jit(solution)/shard_map/pallas_call | solution.py:140
  97.4 0.8 copy-done.7
  98.2 0.8 copy-done.8
  99.0 11.3 %shard_map.71 = (bf16[512,2048]{1,0:T(8,128)(2,1)}, bf16[272,1152]{1,0:T(8,128)(2,1)}, bf16[272,1152]{1,0:T(8,128)(2,1)}) custom-call(f32[3]{0:T(128)} %pad_maximum_fusion.2.scal, bf16[256,1152]{1,0:T(8,128)(2,1)} %copy-done.7, bf16[256,1152]{1,0:T(8,128)(2,1)} %copy-done.8, bf16[512,1152]{1,0:T(8,128)(2,1)} %get-tuple-element.26.refs_1_.refs_2_, ...), custom_call_target="tpu_custom_call" | custom-call | tf_op jit(solution)/shard_map/pallas_call | solution.py:140
  110.3 10.6 %shard_map.75 = (bf16[512,1152]{1,0:T(8,128)(2,1)}, bf16[512,1152]{1,0:T(8,128)(2,1)}) custom-call(bf16[512,2048]{1,0:T(8,128)(2,1)} %get-tuple-element.39.refs_0_, bf16[512,2048]{1,0:T(8,128)(2,1)} %get-tuple-element.40.refs_1_, bf16[512,2048]{1,0:T(8,128)(2,1)} %get-tuple-element.41.refs_2_, bf16[512,2048]{1,0:T(8,128)(2,1)} %get-tuple-element.42.refs_3_, ...), custom_call_target="tpu_custom_call" | custom-call | tf_op jit(solution)/shard_map/pallas_call | solution.py:204
  121.0 0.1 collective-permute-start.16
  121.0 0.1 collective-permute-start.12
  121.1 3.2 %collective-permute-start.7 = (bf16[272,1152]{1,0:T(8,128)(2,1)S(1)}, bf16[272,1152]{1,0:T(8,128)(2,1)S(1)}, u32[]{:S(2)}, u32[]{:S(2)}) collective-permute-start(bf16[272,1152]{1,0:T(8,128)(2,1)S(1)} %copy-done.20), channel_id=1, source_target_pairs={{0,12},{1,13},{2,14},{3,15},{4,0},{5,1},{6,2},{7,3},{8,4},{9,5},{1... | collective-permute-start | bytes 1880072 | tf_op jit(solution)/shard_map/ppermute | solution.py:279
  124.4 10.4 %shard_map.74 = (f32[512,1152]{1,0:T(8,128)}, bf16[512,1152]{1,0:T(8,128)(2,1)}) custom-call(bf16[512,2048]{1,0:T(8,128)(2,1)} %get-tuple-element.39.refs_0_, bf16[512,2048]{1,0:T(8,128)(2,1)} %get-tuple-element.40.refs_1_, bf16[512,2048]{1,0:T(8,128)(2,1)} %get-tuple-element.41.refs_2_, bf16[512,2048]{1,0:T(8,128)(2,1)} %get-tuple-element.42.refs_3_, ...), custom_call_target="tpu_custom_call" | custom-call | tf_op jit(solution)/shard_map/pallas_call | solution.py:204
  134.8 0.1 collective-permute-start.15
  135.0 0.3 add.11
  135.3 3.3 %collective-permute-start.17 = (bf16[512,1152]{1,0:T(8,128)(2,1)S(1)}, bf16[512,1152]{1,0:T(8,128)(2,1)S(1)}, u32[]{:S(2)}, u32[]{:S(2)}) collective-permute-start(bf16[512,1152]{1,0:T(8,128)(2,1)S(1)} %add.11), channel_id=1, source_target_pairs={{0,2},{1,3},{2,0},{3,1},{4,6},{5,7},{6,4},{7,5},{8,10},{9,11},{10,... | collective-permute-start | bytes 3538952 | tf_op jit(solution)/shard_map/ppermute | solution.py:279
  138.6 0.5 collective-permute-done.12
  139.0 0.2 add.10
  139.2 1.5 collective-permute-start.13
  140.7 0.1 collective-permute-start.11
  140.8 0.2 add.9
  140.9 10.7 %collective-permute-done.14.r_ref = bf16[272,1152]{1,0:T(8,128)(2,1)S(1)} collective-permute-done((bf16[272,1152]{1,0:T(8,128)(2,1)}, bf16[272,1152]{1,0:T(8,128)(2,1)S(1)}, u32[]{:S(2)}, u32[]{:S(2)}) %collective-permute-start.14) | collective-permute-done | bytes 626720 | tf_op jit(solution)/shard_map/ppermute | solution.py:279
  151.6 3.6 %collective-permute-start.8 = (bf16[272,1152]{1,0:T(8,128)(2,1)S(1)}, bf16[272,1152]{1,0:T(8,128)(2,1)S(1)}, u32[]{:S(2)}, u32[]{:S(2)}) collective-permute-start(bf16[272,1152]{1,0:T(8,128)(2,1)S(1)} %add.9), channel_id=1, source_target_pairs={{0,12},{1,13},{2,14},{3,15},{4,0},{5,1},{6,2},{7,3},{8,4},{9,5},{1... | collective-permute-start | bytes 1880072 | tf_op jit(solution)/shard_map/ppermute | solution.py:279
  155.2 2.3 %collective-permute-done.13.s_ref = bf16[272,1152]{1,0:T(8,128)(2,1)S(1)} collective-permute-done((bf16[272,1152]{1,0:T(8,128)(2,1)S(1)}, bf16[272,1152]{1,0:T(8,128)(2,1)S(1)}, u32[]{:S(2)}, u32[]{:S(2)}) %collective-permute-start.13) | collective-permute-done | bytes 626720 | tf_op jit(solution)/shard_map/ppermute | solution.py:279
  157.5 0.8 copy-done.16
  158.3 3.3 %shard_map.73 = (bf16[256,1152]{1,0:T(8,128)(2,1)}, f32[8,256]{1,0:T(8,128)}) custom-call(f32[3]{0:T(128)} %pad_maximum_fusion.2.scal, bf16[512,1152]{1,0:T(8,128)(2,1)} %raw.4, f32[512,1152]{1,0:T(8,128)} %get-tuple-element.27.own, f32[8,512]{1,0:T(8,128)} %get-tuple-element.28.loss, bf16[272,1152]{1,0:T(8,128)(2,1)} %copy-done.16, bf16[272,1152]{1,0:T(8,128)(2,1)} %copy-done.14), custom_call_target="tpu_custom_call" | custom-call | tf_op jit(solution)/shard_map/pallas_call | solution.py:243
  161.5 0.7 slice.15
  162.2 7.4 %collective-permute-done.11.r_ref = bf16[272,1152]{1,0:T(8,128)(2,1)S(1)} collective-permute-done((bf16[272,1152]{1,0:T(8,128)(2,1)S(1)}, bf16[272,1152]{1,0:T(8,128)(2,1)S(1)}, u32[]{:S(2)}, u32[]{:S(2)}) %collective-permute-start.11) | collective-permute-done | bytes 626720 | tf_op jit(solution)/shard_map/ppermute | solution.py:279
  169.6 0.8 copy-done.15
  170.5 0.8 copy-done.17
  171.3 3.2 %shard_map.72 = (bf16[256,1152]{1,0:T(8,128)(2,1)}, f32[8,256]{1,0:T(8,128)}) custom-call(f32[3]{0:T(128)} %pad_maximum_fusion.2.scal, bf16[512,1152]{1,0:T(8,128)(2,1)} %raw.4, f32[512,1152]{1,0:T(8,128)} %get-tuple-element.27.own, f32[8,512]{1,0:T(8,128)} %get-tuple-element.28.loss, bf16[272,1152]{1,0:T(8,128)(2,1)} %copy-done.17, bf16[272,1152]{1,0:T(8,128)(2,1)} %copy-done.15), custom_call_target="tpu_custom_call" | custom-call | tf_op jit(solution)/shard_map/pallas_call | solution.py:243
  174.5 0.7 slice.14
  175.2 0.6 pad_maximum_fusion.1
  175.8 2.2 %pad_maximum_fusion = bf16[512,1152]{1,0:T(8,128)(2,1)} fusion(bf16[256,1152]{1,0:T(8,128)(2,1)S(1)} %copy-done.18, bf16[256,1152]{1,0:T(8,128)(2,1)} %get-tuple-element.37), kind=kLoop, calls=%fused_computation | loop fusion | flops 2359296 | bytes 2359296 | tf_op jit(solution)/shard_map/concatenate | solution.py:315
  178.0 1.0 copy-done.9
  179.0 0.4 copy-done.10
  179.4 4.1 %shard_map.76 = bf16[512,1152]{1,0:T(8,128)(2,1)} custom-call(f32[3]{0:T(128)} %pad_maximum_fusion.2.scal, bf16[512,1152]{1,0:T(8,128)(2,1)} %raw.5, f32[512,1152]{1,0:T(8,128)} %get-tuple-element.43.own, bf16[512,1152]{1,0:T(8,128)(2,1)} %copy-done.9, bf16[512,1152]{1,0:T(8,128)(2,1)} %copy-done.10), custom_call_target="tpu_custom_call" | custom-call | tf_op jit(solution)/shard_map/pallas_call | solution.py:261
  (49 shorter events, 0.2 us)
Async XLA Ops:
  3.6 29.5 %collective-permute-start.1 = (bf16[512,1152]{1,0:T(8,128)(2,1)}, bf16[512,1152]{1,0:T(8,128)(2,1)S(1)}, u32[]{:S(2)}, u32[]{:S(2)}) collective-permute-start(bf16[512,1152]{1,0:T(8,128)(2,1)} %get-tuple-element.26.refs_1_.refs_2_), channel_id=1, source_target_pairs={{0,2},{1,3},{2,0},{3,1},{4,6},{5,7},{6,4},{7,5},{8,10},{9,11},{10,... | collective-permute-start | bytes 3538952 | tf_op jit(solution)/shard_map/ppermute | solution.py:279
  6.9 47.5 %collective-permute-start = (bf16[512,1152]{1,0:T(8,128)(2,1)}, bf16[512,1152]{1,0:T(8,128)(2,1)S(1)}, u32[]{:S(2)}, u32[]{:S(2)}) collective-permute-start(bf16[512,1152]{1,0:T(8,128)(2,1)} %get-tuple-element.26.refs_1_.refs_2_), channel_id=1, source_target_pairs={{0,1},{1,0},{2,3},{3,2},{4,5},{5,4},{6,7},{7,6},{8,9},{9,8},{10,11... | collective-permute-start | bytes 3538952 | tf_op jit(solution)/shard_map/ppermute | solution.py:279
  33.0 26.7 %copy-start = (bf16[512,1152]{1,0:T(8,128)(2,1)}, bf16[512,1152]{1,0:T(8,128)(2,1)S(1)}, u32[]{:S(2)}) copy-start(bf16[512,1152]{1,0:T(8,128)(2,1)S(1)} %collective-permute-done.1.refs_3_.refs_4_) | copy-start | bytes 3538948
  33.0 26.7 %collective-permute-start.2 = (bf16[512,1152]{1,0:T(8,128)(2,1)S(1)}, bf16[512,1152]{1,0:T(8,128)(2,1)S(1)}, u32[]{:S(2)}, u32[]{:S(2)}) collective-permute-start(bf16[512,1152]{1,0:T(8,128)(2,1)S(1)} %collective-permute-done.1.refs_3_.refs_4_), channel_id=1, source_target_pairs={{0,1},{1,0},{2,3},{3,2},{4,5},{5,4},{6,7},{7,6},{8,9},{9,8},{10,11... | collective-permute-start | bytes 3538952 | tf_op jit(solution)/shard_map/ppermute | solution.py:279
  33.0 18.1 %collective-permute-start.3 = (bf16[256,1152]{1,0:T(8,128)(2,1)S(1)}, bf16[256,1152]{1,0:T(8,128)(2,1)S(1)}, u32[]{:S(2)}, u32[]{:S(2)}) collective-permute-start(bf16[256,1152]{1,0:T(8,128)(2,1)S(1)} %get-tuple-element.48), channel_id=1, source_target_pairs={{0,4},{1,5},{2,6},{3,7},{4,8},{5,9},{6,10},{7,11},{8,12},{9,13},{1... | collective-permute-start | bytes 1769480 | tf_op jit(solution)/shard_map/ppermute | solution.py:279
  35.0 16.1 %collective-permute-start.4 = (bf16[256,1152]{1,0:T(8,128)(2,1)S(1)}, bf16[256,1152]{1,0:T(8,128)(2,1)S(1)}, u32[]{:S(2)}, u32[]{:S(2)}) collective-permute-start(bf16[256,1152]{1,0:T(8,128)(2,1)S(1)} %get-tuple-element.47), channel_id=1, source_target_pairs={{0,12},{1,13},{2,14},{3,15},{4,0},{5,1},{6,2},{7,3},{8,4},{9,5},{1... | collective-permute-start | bytes 1769480 | tf_op jit(solution)/shard_map/ppermute | solution.py:279
  51.1 21.4 %copy-start.3 = (bf16[256,1152]{1,0:T(8,128)(2,1)}, bf16[256,1152]{1,0:T(8,128)(2,1)S(1)}, u32[]{:S(2)}) copy-start(bf16[256,1152]{1,0:T(8,128)(2,1)S(1)} %collective-permute-done.3.refs_0_.refs_5_) | copy-start | bytes 1769476
  51.1 32.8 %collective-permute-start.5 = (bf16[256,1152]{1,0:T(8,128)(2,1)S(1)}, bf16[256,1152]{1,0:T(8,128)(2,1)S(1)}, u32[]{:S(2)}, u32[]{:S(2)}) collective-permute-start(bf16[256,1152]{1,0:T(8,128)(2,1)S(1)} %collective-permute-done.3.refs_0_.refs_5_), channel_id=1, source_target_pairs={{0,4},{1,5},{2,6},{3,7},{4,8},{5,9},{6,10},{7,11},{8,12},{9,13},{1... | collective-permute-start | bytes 1769480 | tf_op jit(solution)/shard_map/ppermute | solution.py:279
  51.1 21.4 %copy-start.4 = (bf16[256,1152]{1,0:T(8,128)(2,1)}, bf16[256,1152]{1,0:T(8,128)(2,1)S(1)}, u32[]{:S(2)}) copy-start(bf16[256,1152]{1,0:T(8,128)(2,1)S(1)} %collective-permute-done.4.refs_1_.refs_6_) | copy-start | bytes 1769476
  51.1 32.8 %collective-permute-start.6 = (bf16[256,1152]{1,0:T(8,128)(2,1)S(1)}, bf16[256,1152]{1,0:T(8,128)(2,1)S(1)}, u32[]{:S(2)}, u32[]{:S(2)}) collective-permute-start(bf16[256,1152]{1,0:T(8,128)(2,1)S(1)} %collective-permute-done.4.refs_1_.refs_6_), channel_id=1, source_target_pairs={{0,12},{1,13},{2,14},{3,15},{4,0},{5,1},{6,2},{7,3},{8,4},{9,5},{1... | collective-permute-start | bytes 1769480 | tf_op jit(solution)/shard_map/ppermute | solution.py:279
  54.4 43.0 %collective-permute-start.9 = (bf16[256,1152]{1,0:T(8,128)(2,1)S(1)}, bf16[256,1152]{1,0:T(8,128)(2,1)S(1)}, u32[]{:S(2)}, u32[]{:S(2)}) collective-permute-start(bf16[256,1152]{1,0:T(8,128)(2,1)S(1)} %get-tuple-element.47), channel_id=1, source_target_pairs={{0,4},{1,5},{2,6},{3,7},{4,8},{5,9},{6,10},{7,11},{8,12},{9,13},{1... | collective-permute-start | bytes 1769480 | tf_op jit(solution)/shard_map/ppermute | solution.py:279
  54.4 5.3 %copy-start.1 = (bf16[512,1152]{1,0:T(8,128)(2,1)}, bf16[512,1152]{1,0:T(8,128)(2,1)S(1)}, u32[]{:S(2)}) copy-start(bf16[512,1152]{1,0:T(8,128)(2,1)S(1)} %collective-permute-done.refs_2_.refs_3_) | copy-start | bytes 3538948
  54.4 43.0 %collective-permute-start.10 = (bf16[256,1152]{1,0:T(8,128)(2,1)S(1)}, bf16[256,1152]{1,0:T(8,128)(2,1)S(1)}, u32[]{:S(2)}, u32[]{:S(2)}) collective-permute-start(bf16[256,1152]{1,0:T(8,128)(2,1)S(1)} %get-tuple-element.48), channel_id=1, source_target_pairs={{0,12},{1,13},{2,14},{3,15},{4,0},{5,1},{6,2},{7,3},{8,4},{9,5},{1... | collective-permute-start | bytes 1769480 | tf_op jit(solution)/shard_map/ppermute | solution.py:279
  59.7 1.0 copy-start.2
  83.9 0.8 copy-start.5
  84.7 0.8 copy-start.6
  97.3 0.8 copy-start.7
  98.2 0.8 copy-start.8
  110.3 10.8 %copy-start.20 = (bf16[272,1152]{1,0:T(8,128)(2,1)S(1)}, bf16[272,1152]{1,0:T(8,128)(2,1)}, u32[]{:S(2)}) copy-start(bf16[272,1152]{1,0:T(8,128)(2,1)} %get-tuple-element.30) | copy-start | bytes 1880068
  121.0 14.0 %collective-permute-start.16 = (bf16[512,1152]{1,0:T(8,128)(2,1)}, bf16[512,1152]{1,0:T(8,128)(2,1)S(1)}, u32[]{:S(2)}, u32[]{:S(2)}) collective-permute-start(bf16[512,1152]{1,0:T(8,128)(2,1)} %get-tuple-element.46), channel_id=1, source_target_pairs={{0,1},{1,0},{2,3},{3,2},{4,5},{5,4},{6,7},{7,6},{8,9},{9,8},{10,11... | collective-permute-start | bytes 3538952 | tf_op jit(solution)/shard_map/ppermute | solution.py:279
  121.0 18.0 %collective-permute-start.12 = (bf16[272,1152]{1,0:T(8,128)(2,1)}, bf16[272,1152]{1,0:T(8,128)(2,1)S(1)}, u32[]{:S(2)}, u32[]{:S(2)}) collective-permute-start(bf16[272,1152]{1,0:T(8,128)(2,1)} %get-tuple-element.34), channel_id=1, source_target_pairs={{0,4},{1,5},{2,6},{3,7},{4,8},{5,9},{6,10},{7,11},{8,12},{9,13},{1... | collective-permute-start | bytes 1880072 | tf_op jit(solution)/shard_map/ppermute | solution.py:279
  121.1 19.5 %collective-permute-start.7 = (bf16[272,1152]{1,0:T(8,128)(2,1)S(1)}, bf16[272,1152]{1,0:T(8,128)(2,1)S(1)}, u32[]{:S(2)}, u32[]{:S(2)}) collective-permute-start(bf16[272,1152]{1,0:T(8,128)(2,1)S(1)} %copy-done.20), channel_id=1, source_target_pairs={{0,12},{1,13},{2,14},{3,15},{4,0},{5,1},{6,2},{7,3},{8,4},{9,5},{1... | collective-permute-start | bytes 1880072 | tf_op jit(solution)/shard_map/ppermute | solution.py:279
  124.4 10.6 %copy-start.11 = (bf16[512,1152]{1,0:T(8,128)(2,1)S(1)}, bf16[512,1152]{1,0:T(8,128)(2,1)}, u32[]{:S(2)}) copy-start(bf16[512,1152]{1,0:T(8,128)(2,1)} %get-tuple-element.45) | copy-start | bytes 3538948
  124.4 27.2 %collective-permute-start.14 = (bf16[272,1152]{1,0:T(8,128)(2,1)}, bf16[272,1152]{1,0:T(8,128)(2,1)S(1)}, u32[]{:S(2)}, u32[]{:S(2)}) collective-permute-start(bf16[272,1152]{1,0:T(8,128)(2,1)} %get-tuple-element.35), channel_id=1, source_target_pairs={{0,12},{1,13},{2,14},{3,15},{4,0},{5,1},{6,2},{7,3},{8,4},{9,5},{1... | collective-permute-start | bytes 1880072 | tf_op jit(solution)/shard_map/ppermute | solution.py:279
  134.8 43.1 %collective-permute-start.15 = (bf16[512,1152]{1,0:T(8,128)(2,1)}, bf16[512,1152]{1,0:T(8,128)(2,1)S(1)}, u32[]{:S(2)}, u32[]{:S(2)}) collective-permute-start(bf16[512,1152]{1,0:T(8,128)(2,1)} %get-tuple-element.44), channel_id=1, source_target_pairs={{0,1},{1,0},{2,3},{3,2},{4,5},{5,4},{6,7},{7,6},{8,9},{9,8},{10,11... | collective-permute-start | bytes 3538952 | tf_op jit(solution)/shard_map/ppermute | solution.py:279
  135.0 4.0 %copy-start.13 = (bf16[272,1152]{1,0:T(8,128)(2,1)S(1)}, bf16[272,1152]{1,0:T(8,128)(2,1)}, u32[]{:S(2)}) copy-start(bf16[272,1152]{1,0:T(8,128)(2,1)} %get-tuple-element.33) | copy-start | bytes 1880068
  135.3 5.4 %copy-start.19 = (bf16[272,1152]{1,0:T(8,128)(2,1)S(1)}, bf16[272,1152]{1,0:T(8,128)(2,1)}, u32[]{:S(2)}) copy-start(bf16[272,1152]{1,0:T(8,128)(2,1)} %get-tuple-element.31) | copy-start | bytes 1880068
  135.3 5.5 %copy-start.12 = (bf16[272,1152]{1,0:T(8,128)(2,1)S(1)}, bf16[272,1152]{1,0:T(8,128)(2,1)}, u32[]{:S(2)}) copy-start(bf16[272,1152]{1,0:T(8,128)(2,1)} %get-tuple-element.29) | copy-start | bytes 1880068
  135.3 42.7 %collective-permute-start.17 = (bf16[512,1152]{1,0:T(8,128)(2,1)S(1)}, bf16[512,1152]{1,0:T(8,128)(2,1)S(1)}, u32[]{:S(2)}, u32[]{:S(2)}) collective-permute-start(bf16[512,1152]{1,0:T(8,128)(2,1)S(1)} %add.11), channel_id=1, source_target_pairs={{0,2},{1,3},{2,0},{3,1},{4,6},{5,7},{6,4},{7,5},{8,10},{9,11},{10,... | collective-permute-start | bytes 3538952 | tf_op jit(solution)/shard_map/ppermute | solution.py:279
  139.2 18.3 %collective-permute-start.13 = (bf16[272,1152]{1,0:T(8,128)(2,1)S(1)}, bf16[272,1152]{1,0:T(8,128)(2,1)S(1)}, u32[]{:S(2)}, u32[]{:S(2)}) collective-permute-start(bf16[272,1152]{1,0:T(8,128)(2,1)S(1)} %add.10), channel_id=1, source_target_pairs={{0,4},{1,5},{2,6},{3,7},{4,8},{5,9},{6,10},{7,11},{8,12},{9,13},{1... | collective-permute-start | bytes 1880072 | tf_op jit(solution)/shard_map/ppermute | solution.py:279
  140.7 29.0 %collective-permute-start.11 = (bf16[272,1152]{1,0:T(8,128)(2,1)S(1)}, bf16[272,1152]{1,0:T(8,128)(2,1)S(1)}, u32[]{:S(2)}, u32[]{:S(2)}) collective-permute-start(bf16[272,1152]{1,0:T(8,128)(2,1)S(1)} %copy-done.19), channel_id=1, source_target_pairs={{0,4},{1,5},{2,6},{3,7},{4,8},{5,9},{6,10},{7,11},{8,12},{9,13},{1... | collective-permute-start | bytes 1880072 | tf_op jit(solution)/shard_map/ppermute | solution.py:279
  151.6 5.9 %copy-start.14 = (bf16[272,1152]{1,0:T(8,128)(2,1)}, bf16[272,1152]{1,0:T(8,128)(2,1)S(1)}, u32[]{:S(2)}) copy-start(bf16[272,1152]{1,0:T(8,128)(2,1)S(1)} %collective-permute-done.14.r_ref) | copy-start | bytes 1880068
  151.6 18.0 %collective-permute-start.8 = (bf16[272,1152]{1,0:T(8,128)(2,1)S(1)}, bf16[272,1152]{1,0:T(8,128)(2,1)S(1)}, u32[]{:S(2)}, u32[]{:S(2)}) collective-permute-start(bf16[272,1152]{1,0:T(8,128)(2,1)S(1)} %add.9), channel_id=1, source_target_pairs={{0,12},{1,13},{2,14},{3,15},{4,0},{5,1},{6,2},{7,3},{8,4},{9,5},{1... | collective-permute-start | bytes 1880072 | tf_op jit(solution)/shard_map/ppermute | solution.py:279
  157.5 0.8 copy-start.16
  162.2 13.6 %copy-start.18 = (bf16[256,1152]{1,0:T(8,128)(2,1)S(1)}, bf16[256,1152]{1,0:T(8,128)(2,1)}, u32[]{:S(2)}) copy-start(bf16[256,1152]{1,0:T(8,128)(2,1)} %get-tuple-element.38) | copy-start | bytes 1769476
  169.6 0.8 copy-start.15
  170.5 0.8 copy-start.17
  178.0 1.0 copy-start.9
  178.0 1.4 copy-start.10
